TPU v7x, 256 devices: a whole 4x4x8 slice. The times are simulated.
256 devices in a mesh: tower: 8 (over x, core), peer: 32 (over z, y).
Axes of the slice: x: 4, y: 4, z: 8, core: 2. Of those that a mesh axis runs over, the one named last changes fastest.
Arguments:
- embeddings: bfloat16 [16384, 2048], P('tower', 'peer'), may hold values from -6 to 6
- session_lists: int32 [8, 2048], P('tower'), may hold values from 0 to 2047, each once within a row
- owners: int32 [16384, 1], P(('tower', 'peer')), may hold values from 0 to 7; in each aligned block of 64 rows (0 to 63, 64 to 127, ...) at most 16 rows name the same one
- counts: int32 [16384], P(('tower', 'peer')), may hold values from 1 to 3, as said below
- item_feats: bfloat16 [98304, 256], P(('tower', 'peer')), may hold values from -6 to 6
- cotangent: bfloat16 [98304, 1024], P(('tower', 'peer')), may hold values from -6 to 6
- cross_down: bfloat16 [2048, 256], replicated, may hold values from -0.125 to 0.125
- cross_up: bfloat16 [256, 2048], replicated, may hold values from -0.375 to 0.375
- compress: bfloat16 [2048, 256], replicated, may hold values from -0.125 to 0.125
- over_first: bfloat16 [512, 4096], replicated, may hold values from -0.25 to 0.25
- over_second: bfloat16 [4096, 1024], P('peer'), may hold values from -0.09375 to 0.09375
- over_third: bfloat16 [1024, 1024], replicated, may hold values from -0.1875 to 0.1875
Outputs:
- over_out: bfloat16 [98304, 1024], P(('tower', 'peer'))
- emb_grad: bfloat16 [16384, 2048], P('tower', 'peer')
Inputs may be any that keep to these rules, and one draw needn't show every extreme that they name: `session_lists`: each row is a permutation of the tower's 64 * 32 table rows. `owners`: within the 64 sessions of one device, no tower owns more than 16 of them. `counts`: the first session of every device has 3 samples and the second has one.
All inputs are finite; a program needn't handle non-finite values.
Results may differ from a plain program's by a relative error of at most 0.02.
Values may be sent and summed in bfloat16 or wider, within the bound.
A program may use at most 128 MiB of HBM per device.

v0:
```python
import jax
import jax.numpy as jnp
from jax import lax
from jax.sharding import PartitionSpec as P

MOSTC = 3


def silu_slope(pre):
    sigma = jax.nn.sigmoid(pre)
    return sigma * (1.0 + pre * (1.0 - sigma))


def times_t(left, right):
    return lax.dot_general(
        left, right, (((1,), (1,)), ((), ())), preferred_element_type=jnp.float32
    )


def body(
    embeddings,
    session_lists,
    owners,
    counts,
    item_feats,
    cotangent,
    cross_down,
    cross_up,
    compress,
    over_first,
    over_second,
    over_third,
):
    towers = lax.axis_size("tower")
    comp_width = compress.shape[1]
    grid_rows = item_feats.shape[0]
    slots = grid_rows // (towers * MOSTC)
    order = session_lists[0]
    picked = jnp.take(embeddings, order, axis=0)
    session_rows = lax.all_to_all(picked, "peer", split_axis=0, concat_axis=1, tiled=True)
    low = jnp.dot(session_rows, cross_down, preferred_element_type=jnp.float32).astype(jnp.bfloat16)
    lift = jnp.dot(low, cross_up, preferred_element_type=jnp.float32)
    rows_wide = session_rows.astype(jnp.float32)
    crossed = (rows_wide * lift + rows_wide).astype(jnp.bfloat16)
    compressed = jnp.dot(crossed, compress, preferred_element_type=jnp.float32).astype(jnp.bfloat16)
    owner_list = owners[:, 0]
    choose = (owner_list[:, None] == jnp.arange(towers, dtype=jnp.int32)[None, :]).astype(jnp.int32)
    earlier = jnp.cumsum(choose, axis=0) - choose
    position = jnp.sum(choose * earlier, axis=1)
    target = owner_list * slots + position
    dispatch = (target[:, None] == jnp.arange(towers * slots, dtype=jnp.int32)[None, :]).astype(
        jnp.int32
    )
    dispatch_half = dispatch.astype(jnp.bfloat16)
    send_rows = lax.dot_general(
        dispatch_half, compressed, (((0,), (0,)), ((), ())), preferred_element_type=jnp.float32
    ).astype(jnp.bfloat16)
    send_counts = jnp.sum(dispatch * counts[:, None], axis=0)
    repeated = jnp.broadcast_to(send_rows[:, None, :], (towers * slots, MOSTC, comp_width))
    repeated = repeated.reshape(towers, slots * MOSTC, comp_width)
    got_rows, got_counts = (
        lax.all_to_all(repeated, "tower", split_axis=0, concat_axis=0, tiled=True),
        lax.all_to_all(
            send_counts.reshape(towers, slots), "tower", split_axis=0, concat_axis=0, tiled=True
        ),
    )
    expanded = got_rows.reshape(grid_rows, comp_width)
    live = (
        jnp.arange(MOSTC, dtype=jnp.int32)[None, :] < got_counts.reshape(towers * slots)[:, None]
    ).astype(jnp.float32)
    live = live.reshape(grid_rows)
    inputs = jnp.concatenate([expanded, item_feats], axis=1)
    pre_first = jnp.dot(inputs, over_first, preferred_element_type=jnp.float32)
    hidden_first = jax.nn.silu(pre_first).astype(jnp.bfloat16)
    pre_second = jnp.dot(
        hidden_first,
        lax.all_gather(over_second, "peer", axis=0, tiled=True),
        preferred_element_type=jnp.float32,
    )
    hidden_second = jax.nn.silu(pre_second).astype(jnp.bfloat16)
    over_out = (
        jnp.dot(hidden_second, over_third, preferred_element_type=jnp.float32) * live[:, None]
    ).astype(jnp.bfloat16)
    masked = cotangent * live[:, None].astype(jnp.bfloat16)
    grad_second = (times_t(masked, over_third) * silu_slope(pre_second)).astype(jnp.bfloat16)
    back_first = times_t(grad_second, lax.all_gather(over_second, "peer", axis=0, tiled=True))
    grad_first = (back_first * silu_slope(pre_first)).astype(jnp.bfloat16)
    sample_grad = times_t(grad_first, over_first[:comp_width]).astype(jnp.bfloat16)
    returned = lax.all_to_all(
        sample_grad.reshape(towers, slots * MOSTC, comp_width),
        "tower",
        split_axis=0,
        concat_axis=0,
        tiled=True,
    )
    slot_grad = jnp.sum(
        returned.astype(jnp.float32).reshape(towers * slots, MOSTC, comp_width), axis=1
    ).astype(jnp.bfloat16)
    session_grad = jnp.dot(dispatch_half, slot_grad, preferred_element_type=jnp.float32).astype(
        jnp.bfloat16
    )
    grad_crossed = times_t(session_grad, compress).astype(jnp.bfloat16)
    grad_lift = (grad_crossed.astype(jnp.float32) * rows_wide).astype(jnp.bfloat16)
    grad_low = times_t(grad_lift, cross_up).astype(jnp.bfloat16)
    grad_rows = (
        grad_crossed.astype(jnp.float32) * (lift + 1.0) + times_t(grad_low, cross_down)
    ).astype(jnp.bfloat16)
    columns_back = lax.all_to_all(grad_rows, "peer", split_axis=1, concat_axis=0, tiled=True)
    emb_grad = jnp.zeros_like(embeddings).at[order].set(columns_back)
    return (over_out, emb_grad)


def solution(mesh):
    return jax.shard_map(
        body,
        mesh=mesh,
        in_specs=(
            P("tower", "peer"),
            P("tower", None),
            P(("tower", "peer"), None),
            P(("tower", "peer")),
            P(("tower", "peer"), None),
            P(("tower", "peer"), None),
            P(),
            P(),
            P(),
            P(),
            P("peer", None),
            P(),
        ),
        out_specs=(P(("tower", "peer"), None), P("tower", "peer")),
        check_vma=False,
    )
```

profile of v0, /device:TPU:32, one launch (start us, length us, event | category | flops | bytes accessed | tf_op | source)
XLA Modules:
  0.0 187.4 jit_solution(9144501375350728294)
XLA Ops:
  7.2 0.0 copy-start
  7.2 0.0 all-gather.2.cloned.1.call-start
  7.2 0.7 all-gather.2.cloned.1.call-update
  7.9 0.7 fusion.25
  8.6 0.1 reduce_window_sum.11
  8.7 0.8 select_reduce_fusion.1
  9.6 0.7 fusion.29
  10.2 0.7 select_reduce_fusion
  11.0 0.7 all_to_all.42
  11.7 4.3 %all-to-all-start.2 = ((s32[8,1,16]{2,1,0:T(1,128)}), s32[8,1,16]{2,1,0:T(1,128)S(1)}, u32[]{:S(2)}, u32[]{:S(2)}) async-start(s32[8,1,16]{2,1,0:T(1,128)} %bitcast.8), calls=%async_computation.2 | async-start | bytes 8192 | tf_op jit(solution)/shard_map/all_to_all | solution.py:63
  16.0 1.2 copy.28
  17.2 0.5 broadcast.66
  17.7 1.3 reduce.7
  19.0 0.1 squeeze.6
  19.1 0.7 compare_select_fusion
  19.8 6.2 %gather_fusion = bf16[2048,64]{1,0:T(8,128)(2,1)S(1)} fusion(bf16[2048,64]{1,0:T(8,128)(2,1)S(1)} %copy.28, s32[2048]{0:T(1024)S(1)} %broadcast_clamp_fusion), kind=kCustom, calls=%fused_computation | custom fusion | bytes 532480 | tf_op jit(solution)/shard_map/jit(_take)/gather | solution.py:39
  26.0 0.3 broadcast_select_fusion
  26.3 1.1 reshape.142
  27.4 0.0 all-to-all-done.2
  27.4 11.4 %all-to-all-start = ((bf16[32,2,2048]{2,1,0:T(2,128)(2,1)}), bf16[32,2,2048]{2,1,0:T(2,128)(2,1)S(1)}, u32[]{:S(2)}, u32[]{:S(2)}) async-start(bf16[32,2,2048]{2,1,0:T(2,128)(2,1)} %reshape.142), calls=%async_computation | async-start | bytes 524288 | tf_op jit(solution)/shard_map/all_to_all | solution.py:40
  38.8 0.6 reduce.8
  39.4 0.1 lt.53
  39.5 14.4 %all-to-all-done = bf16[32,2,2048]{2,1,0:T(2,128)(2,1)S(1)} async-done(((bf16[32,2,2048]{2,1,0:T(2,128)(2,1)}), bf16[32,2,2048]{2,1,0:T(2,128)(2,1)S(1)}, u32[]{:S(2)}, u32[]{:S(2)}) %all-to-all-start) | async-done | bytes 262176 | tf_op jit(solution)/shard_map/all_to_all | solution.py:40
  53.9 0.4 reshape.143
  54.3 0.3 copy.29
  54.6 0.5 all_to_all.40
  55.1 0.0 copy-start.1
  55.1 2.4 %fusion.8 = f32[64,2048]{1,0:T(8,128)S(1)} fusion(bf16[256,2048]{1,0:T(8,128)(2,1)} %param.19, bf16[64,2048]{1,0:T(8,128)(2,1)S(1)} %all_to_all.40, bf16[2048,256]{1,0:T(8,128)(2,1)} %param.18), kind=kOutput, calls=%fused_computation.22 | convolution fusion | flops 134234112 | bytes 2883584 | tf_op jit(solution)/shard_map/dot_general | solution.py:42
  57.5 1.7 convolution_convert_fusion.1
  59.2 0.1 broadcast_in_dim.16
  59.2 0.8 reshape.102
  60.1 4.5 %all-to-all-start.1 = ((bf16[8,48,256]{2,1,0:T(8,128)(2,1)}), bf16[8,48,256]{2,1,0:T(8,128)(2,1)S(1)}, u32[]{:S(2)}, u32[]{:S(2)}) async-start(bf16[8,48,256]{2,1,0:T(8,128)(2,1)} %reshape.102), calls=%async_computation.1 | async-start | bytes 393216 | tf_op jit(solution)/shard_map/all_to_all | solution.py:62
  64.6 0.1 fusion.24
  64.7 0.2 reshape.107
  64.9 6.5 %all-to-all-done.1 = bf16[8,48,256]{2,1,0:T(8,128)(2,1)S(1)} async-done(((bf16[8,48,256]{2,1,0:T(8,128)(2,1)}), bf16[8,48,256]{2,1,0:T(8,128)(2,1)S(1)}, u32[]{:S(2)}, u32[]{:S(2)}) %all-to-all-start.1) | async-done | bytes 196640 | tf_op jit(solution)/shard_map/all_to_all | solution.py:62
  71.4 0.0 copy-done.1
  71.4 6.7 %fusion.13 = f32[384,4096]{1,0:T(8,128)} fusion(bf16[512,4096]{1,0:T(8,128)(2,1)} %param.21, bf16[384,256]{1,0:T(8,128)(2,1)S(1)} %copy-done.1, bf16[384,256]{1,0:T(8,128)(2,1)S(1)} %bitcast.39), kind=kOutput, calls=%fused_computation.30 | convolution fusion | flops 1611399168 | bytes 10878976 | tf_op jit(solution)/shard_map/dot_general | solution.py:73
  78.1 34.4 %all-gather.2.cloned.1.call-done = bf16[4096,1024]{1,0:T(8,128)(2,1)} async-done(((bf16[128,1024]{1,0:T(8,128)(2,1)}), bf16[4096,1024]{1,0:T(8,128)(2,1)}) %all-gather.2.cloned.1.call-update) | async-done | bytes 8388624 | tf_op jit(solution)/shard_map/all_gather | solution.py:77
  112.5 0.0 copy-start.2
  112.5 8.1 %fusion = f32[384,1024]{1,0:T(8,128)S(1)} fusion(bf16[4096,1024]{1,0:T(8,128)(2,1)} %all-gather.2.cloned.1.call-done, f32[384,4096]{1,0:T(8,128)} %fusion.13), kind=kOutput, calls=%fused_computation.5 | convolution fusion | flops 3229089792 | bytes 16252928 | tf_op jit(solution)/shard_map/dot_general | solution.py:75
  120.7 0.0 copy-start.3
  120.7 1.2 copy-done.3
  121.8 0.0 copy-done
  121.8 0.0 copy-done.2
  121.8 2.1 %multiply_convert_fusion.3 = bf16[384,1024]{1,0:T(8,128)(2,1)} fusion(f32[384,1024]{1,0:T(8,128)S(1)} %fusion, bf16[1024,1024]{1,0:T(8,128)(2,1)S(1)} %copy-done, bf16[384,1024]{1,0:T(8,128)(2,1)S(1)} %copy-done.2, bf16[384]{0:T(512)(128)(2,1)S(1)} %convert_element_type.100), kind=kOutput, calls=%fused_computation.12 | convolution fusion | flops 809238528 | bytes 5243648 | tf_op jit(solution)/shard_map/dot_general | solution.py:15
  124.0 10.5 %fusion.5 = bf16[384,256]{1,0:T(8,128)(2,1)S(1)} fusion(bf16[512,4096]{1,0:T(8,128)(2,1)} %param.21, f32[384,4096]{1,0:T(8,128)} %fusion.13, bf16[384,1024]{1,0:T(8,128)(2,1)} %multiply_convert_fusion.3, bf16[4096,1024]{1,0:T(8,128)(2,1)} %all-gather.2.cloned.1.call-done), kind=kOutput, calls=%fused_computation.16 | convolution fusion | flops 4040785920 | bytes 17760256 | tf_op jit(solution)/shard_map/dot_general | solution.py:15
  134.5 10.9 %all_to_all.54 = bf16[8,48,256]{2,1,0:T(8,128)(2,1)S(1)} all-to-all(bf16[8,48,256]{2,1,0:T(8,128)(2,1)S(1)} %bitcast.41), channel_id=1, replica_groups=mesh['tower'=8,'peer'=32] {'tower'}, dimensions={0} | all-to-all | bytes 393216 | tf_op jit(solution)/shard_map/all_to_all | solution.py:89
  145.4 0.1 reshape.105
  145.5 0.3 reduce
  145.9 1.8 fusion.2
  147.6 3.5 %fusion.1 = bf16[64,2048]{1,0:T(8,128)(2,1)} fusion(bf16[2048,256]{1,0:T(8,128)(2,1)} %param.18, bf16[256,2048]{1,0:T(8,128)(2,1)} %param.19, f32[64,2048]{1,0:T(8,128)S(1)} %fusion.2, f32[64,2048]{1,0:T(8,128)S(1)} %fusion.8, bf16[64,2048]{1,0:T(8,128)(2,1)S(1)} %all_to_all.40), kind=kOutput, calls=%fused_computation.7 | convolution fusion | flops 135151616 | bytes 3670016 | tf_op jit(solution)/shard_map/dot_general | solution.py:15
  151.2 1.5 all_to_all.45
  152.6 0.2 copy.34
  152.8 1.1 reshape.144
  153.9 7.6 %all-to-all-start.4 = ((bf16[32,2,2048]{2,1,0:T(2,128)(2,1)}), bf16[32,2,2048]{2,1,0:T(2,128)(2,1)S(1)}, u32[]{:S(2)}, u32[]{:S(2)}) async-start(bf16[32,2,2048]{2,1,0:T(2,128)(2,1)} %reshape.144), calls=%async_computation.4 | async-start | bytes 524288 | tf_op jit(solution)/shard_map/all_to_all | solution.py:108
  161.6 3.3 %multiply_convert_fusion.4 = bf16[384,1024]{1,0:T(8,128)(2,1)} fusion(bf16[1024,1024]{1,0:T(8,128)(2,1)S(1)} %copy-done, f32[384,1024]{1,0:T(8,128)} %copy-done.3, f32[384]{0:T(512)S(1)} %reshape.107), kind=kOutput, calls=%fused_computation.13 | convolution fusion | flops 808058880 | bytes 4457984 | tf_op jit(solution)/shard_map/dot_general | solution.py:82
  164.9 8.5 %all-to-all-done.4 = bf16[32,2,2048]{2,1,0:T(2,128)(2,1)S(1)} async-done(((bf16[32,2,2048]{2,1,0:T(2,128)(2,1)}), bf16[32,2,2048]{2,1,0:T(2,128)(2,1)S(1)}, u32[]{:S(2)}, u32[]{:S(2)}) %all-to-all-start.4) | async-done | bytes 262176 | tf_op jit(solution)/shard_map/all_to_all | solution.py:108
  173.4 0.4 reshape.145
  173.8 5.9 %scatter_custom_fusion = bf16[2048,64]{1,0:T(8,128)(2,1)S(1)} fusion(s32[2048]{0:T(1024)S(1)} %bitcast.43, bf16[2048,64]{1,0:T(8,128)(2,1)S(1)} %bitcast.40, bf16[]{:T(256)} %constant.36.clone.1), kind=kCustom, calls=%fused_computation.35 | custom fusion | bytes 262146 | tf_op jit(solution)/shard_map/scatter | solution.py:109
  179.6 0.9 copy.32
  (3 shorter events, 0.0 us)
Async XLA Ops:
  7.2 114.7 %copy-start = (bf16[1024,1024]{1,0:T(8,128)(2,1)S(1)}, bf16[1024,1024]{1,0:T(8,128)(2,1)}, u32[]{:S(2)}) copy-start(bf16[1024,1024]{1,0:T(8,128)(2,1)} %param.23) | copy-start | bytes 6291460
  7.2 105.4 %all-gather.2.cloned.1.call-start = ((), (), s32[]{:S(2)}) async-start(), calls=%async_computation.5 | async-start | bytes 8650752 | tf_op jit(solution)/shard_map/all_gather | solution.py:77
  11.7 15.8 %all-to-all-start.2 = ((s32[8,1,16]{2,1,0:T(1,128)}), s32[8,1,16]{2,1,0:T(1,128)S(1)}, u32[]{:S(2)}, u32[]{:S(2)}) async-start(s32[8,1,16]{2,1,0:T(1,128)} %bitcast.8), calls=%async_computation.2 | async-start | bytes 8192 | tf_op jit(solution)/shard_map/all_to_all | solution.py:63
  27.4 26.5 %all-to-all-start = ((bf16[32,2,2048]{2,1,0:T(2,128)(2,1)}), bf16[32,2,2048]{2,1,0:T(2,128)(2,1)S(1)}, u32[]{:S(2)}, u32[]{:S(2)}) async-start(bf16[32,2,2048]{2,1,0:T(2,128)(2,1)} %reshape.142), calls=%async_computation | async-start | bytes 524288 | tf_op jit(solution)/shard_map/all_to_all | solution.py:40
  55.1 16.3 %copy-start.1 = (bf16[384,256]{1,0:T(8,128)(2,1)S(1)}, bf16[384,256]{1,0:T(8,128)(2,1)}, u32[]{:S(2)}) copy-start(bf16[384,256]{1,0:T(8,128)(2,1)} %param.16) | copy-start | bytes 589828
  60.1 11.3 %all-to-all-start.1 = ((bf16[8,48,256]{2,1,0:T(8,128)(2,1)}), bf16[8,48,256]{2,1,0:T(8,128)(2,1)S(1)}, u32[]{:S(2)}, u32[]{:S(2)}) async-start(bf16[8,48,256]{2,1,0:T(8,128)(2,1)} %reshape.102), calls=%async_computation.1 | async-start | bytes 393216 | tf_op jit(solution)/shard_map/all_to_all | solution.py:62
  112.5 9.3 %copy-start.2 = (bf16[384,1024]{1,0:T(8,128)(2,1)S(1)}, bf16[384,1024]{1,0:T(8,128)(2,1)}, u32[]{:S(2)}) copy-start(bf16[384,1024]{1,0:T(8,128)(2,1)} %param.17) | copy-start | bytes 2359300
  120.7 1.2 copy-start.3
  153.9 19.5 %all-to-all-start.4 = ((bf16[32,2,2048]{2,1,0:T(2,128)(2,1)}), bf16[32,2,2048]{2,1,0:T(2,128)(2,1)S(1)}, u32[]{:S(2)}, u32[]{:S(2)}) async-start(bf16[32,2,2048]{2,1,0:T(2,128)(2,1)} %reshape.144), calls=%async_computation.4 | async-start | bytes 524288 | tf_op jit(solution)/shard_map/all_to_all | solution.py:108
Sparse Core Ops, SparseCore 0:
  10.6 101.8 all-gather.1
where the time goes:
time: 188 us; the launch traced here: 187 us
  waiting for transfers between devices  64.6 us (34%)
  matrix products  40.1 us (21%)
  starting transfers between devices  27.8 us (15%)
  local copies, waits for them, and re-layouts  23.3 us (12%)
  between operations  14.2 us (8%)
  blocking collectives  10.9 us (6%)
  other arithmetic  6.42 us (3%)
    all_gather x1, waiting for transfers between devices, body(): lax.all_gather(over_second, 'peer', axis=0, tiled=True)  34.4 us
    dot_general x4, matrix products, times_t(): lax.dot_general(left, right, (((1,), (1,)), ((), ())), preferred_element_...  18 us
    all_to_all x1, waiting for transfers between devices, body(): lax.all_to_all(picked, 'peer', split_axis=0, concat_axis=1, tiled=True)  14.4 us
    all_to_all x1, starting transfers between devices, body(): lax.all_to_all(picked, 'peer', split_axis=0, concat_axis=1, tiled=True)  11.4 us
    all_to_all x1, blocking collectives, body(): lax.all_to_all(sample_grad.reshape(towers, slots * MOSTC, comp_width), 't...  10.9 us
    all_to_all x1, waiting for transfers between devices, body(): lax.all_to_all(grad_rows, 'peer', split_axis=1, concat_axis=0, tiled=True)  8.52 us
    dot_general x1, matrix products, body(): jnp.dot(hidden_first, lax.all_gather(over_second, 'peer', axis=0, tiled=T...  8.1 us
    all_to_all x1, starting transfers between devices, body(): lax.all_to_all(grad_rows, 'peer', split_axis=1, concat_axis=0, tiled=True)  7.63 us
  transfers between devices with their start and end apart: 5, of which 4 were waited for; matrix products, arithmetic and copies ran while one was open for 17% of the time, Pallas kernels for 0%

commit v1 on v0

--- a/solution.py
+++ b/solution.py
@@ -105,7 +105,10 @@
     grad_rows = (
         grad_crossed.astype(jnp.float32) * (lift + 1.0) + times_t(grad_low, cross_down)
     ).astype(jnp.bfloat16)
-    columns_back = lax.all_to_all(grad_rows, "peer", split_axis=1, concat_axis=0, tiled=True)
+    ready = lax.axis_size("peer")
+    all_values = jnp.split(grad_rows, ready, 1)
+    current_arr = lax.all_to_all(jnp.stack(all_values, 0), "peer", 0, 0)
+    columns_back = jnp.concatenate(current_arr, axis=0)
     emb_grad = jnp.zeros_like(embeddings).at[order].set(columns_back)
     return (over_out, emb_grad)
 

time: 188 us -> 189 us (level)
    unnamed x15 -> x46, local copies, waits for them, and re-layouts: 6.71 us -> 8.22 us
where the time goes in v1:
time: 189 us; the launch traced here: 188 us
  waiting for transfers between devices  64.6 us (34%)
  matrix products  40.5 us (21%)
  starting transfers between devices  27.8 us (15%)
  local copies, waits for them, and re-layouts  23.2 us (12%)
  between operations  14.3 us (8%)
  blocking collectives  10.9 us (6%)
  other arithmetic  6.42 us (3%)
    all_gather x1, waiting for transfers between devices, body(): lax.all_gather(over_second, 'peer', axis=0, tiled=True)  34.4 us
    dot_general x4, matrix products, times_t(): lax.dot_general(left, right, (((1,), (1,)), ((), ())), preferred_element_...  18.4 us
    all_to_all x1, waiting for transfers between devices, body(): lax.all_to_all(picked, 'peer', split_axis=0, concat_axis=1, tiled=True)  14.4 us
    all_to_all x1, starting transfers between devices, body(): lax.all_to_all(picked, 'peer', split_axis=0, concat_axis=1, tiled=True)  11.4 us
    all_to_all x1, blocking collectives, body(): lax.all_to_all(sample_grad.reshape(towers, slots * MOSTC, comp_width), 't...  10.9 us
    all_to_all x1, waiting for transfers between devices, body(): current_arr = lax.all_to_all(jnp.stack(all_values, 0), 'peer', 0, 0)  8.52 us
    unnamed x46, local copies, waits for them, and re-layouts  8.22 us
    dot_general x1, matrix products, body(): jnp.dot(hidden_first, lax.all_gather(over_second, 'peer', axis=0, tiled=T...  8.1 us
  transfers between devices with their start and end apart: 5, of which 4 were waited for; matrix products, arithmetic and copies ran while one was open for 17% of the time, Pallas kernels for 0%

profile of v1, /device:TPU:32, one launch (start us, length us, event | category | flops | bytes accessed | tf_op | source)
XLA Modules:
  0.0 187.8 jit_solution(4362244052475032133)
XLA Ops:
  7.2 0.7 all-gather.2.cloned.1.call-update
  7.9 0.7 fusion.25
  8.6 0.1 reduce_window_sum.11
  8.7 0.8 select_reduce_fusion.1
  9.6 0.7 fusion.29
  10.2 0.7 select_reduce_fusion
  11.0 0.7 all_to_all.31
  11.7 4.3 %all-to-all-start.2 = ((s32[8,1,16]{2,1,0:T(1,128)}), s32[8,1,16]{2,1,0:T(1,128)S(1)}, u32[]{:S(2)}, u32[]{:S(2)}) async-start(s32[8,1,16]{2,1,0:T(1,128)} %bitcast.8), calls=%async_computation.2 | async-start | bytes 8192 | tf_op jit(solution)/shard_map/all_to_all | solution.py:63
  16.0 1.2 copy.26
  17.2 0.5 broadcast.66
  17.7 1.3 reduce.7
  19.0 0.1 squeeze.6
  19.1 0.7 compare_select_fusion
  19.8 6.2 %gather_fusion = bf16[2048,64]{1,0:T(8,128)(2,1)S(1)} fusion(bf16[2048,64]{1,0:T(8,128)(2,1)S(1)} %copy.26, s32[2048]{0:T(1024)S(1)} %broadcast_clamp_fusion), kind=kCustom, calls=%fused_computation | custom fusion | bytes 532480 | tf_op jit(solution)/shard_map/jit(_take)/gather | solution.py:39
  26.0 0.3 broadcast_select_fusion
  26.3 1.1 reshape.143
  27.4 11.4 %all-to-all-start = ((bf16[32,2,2048]{2,1,0:T(2,128)(2,1)}), bf16[32,2,2048]{2,1,0:T(2,128)(2,1)S(1)}, u32[]{:S(2)}, u32[]{:S(2)}) async-start(bf16[32,2,2048]{2,1,0:T(2,128)(2,1)} %reshape.143), calls=%async_computation | async-start | bytes 524288 | tf_op jit(solution)/shard_map/all_to_all | solution.py:40
  38.8 0.6 reduce.8
  39.4 0.1 lt.53
  39.5 14.4 %all-to-all-done = bf16[32,2,2048]{2,1,0:T(2,128)(2,1)S(1)} async-done(((bf16[32,2,2048]{2,1,0:T(2,128)(2,1)}), bf16[32,2,2048]{2,1,0:T(2,128)(2,1)S(1)}, u32[]{:S(2)}, u32[]{:S(2)}) %all-to-all-start) | async-done | bytes 262176 | tf_op jit(solution)/shard_map/all_to_all | solution.py:40
  53.9 0.4 reshape.144
  54.3 0.3 copy.27
  54.6 0.5 all_to_all.29
  55.1 2.4 %fusion.8 = f32[64,2048]{1,0:T(8,128)S(1)} fusion(bf16[256,2048]{1,0:T(8,128)(2,1)} %param.19, bf16[64,2048]{1,0:T(8,128)(2,1)S(1)} %all_to_all.29, bf16[2048,256]{1,0:T(8,128)(2,1)} %param.18), kind=kOutput, calls=%fused_computation.22 | convolution fusion | flops 134234112 | bytes 2883584 | tf_op jit(solution)/shard_map/dot_general | solution.py:42
  57.5 1.7 convolution_convert_fusion.1
  59.2 0.8 reshape.102
  60.1 4.5 %all-to-all-start.1 = ((bf16[8,48,256]{2,1,0:T(8,128)(2,1)}), bf16[8,48,256]{2,1,0:T(8,128)(2,1)S(1)}, u32[]{:S(2)}, u32[]{:S(2)}) async-start(bf16[8,48,256]{2,1,0:T(8,128)(2,1)} %reshape.102), calls=%async_computation.1 | async-start | bytes 393216 | tf_op jit(solution)/shard_map/all_to_all | solution.py:62
  64.6 0.1 fusion.24
  64.7 0.2 reshape.108
  64.9 6.5 %all-to-all-done.1 = bf16[8,48,256]{2,1,0:T(8,128)(2,1)S(1)} async-done(((bf16[8,48,256]{2,1,0:T(8,128)(2,1)}), bf16[8,48,256]{2,1,0:T(8,128)(2,1)S(1)}, u32[]{:S(2)}, u32[]{:S(2)}) %all-to-all-start.1) | async-done | bytes 196640 | tf_op jit(solution)/shard_map/all_to_all | solution.py:62
  71.4 6.7 %fusion.13 = f32[384,4096]{1,0:T(8,128)} fusion(bf16[512,4096]{1,0:T(8,128)(2,1)} %param.21, bf16[384,256]{1,0:T(8,128)(2,1)S(1)} %copy-done.1, bf16[384,256]{1,0:T(8,128)(2,1)S(1)} %bitcast.160), kind=kOutput, calls=%fused_computation.30 | convolution fusion | flops 1611399168 | bytes 10878976 | tf_op jit(solution)/shard_map/dot_general | solution.py:73
  78.1 34.4 %all-gather.2.cloned.1.call-done = bf16[4096,1024]{1,0:T(8,128)(2,1)} async-done(((bf16[128,1024]{1,0:T(8,128)(2,1)}), bf16[4096,1024]{1,0:T(8,128)(2,1)}) %all-gather.2.cloned.1.call-update) | async-done | bytes 8388624 | tf_op jit(solution)/shard_map/all_gather | solution.py:77
  112.5 8.1 %fusion = f32[384,1024]{1,0:T(8,128)S(1)} fusion(bf16[4096,1024]{1,0:T(8,128)(2,1)} %all-gather.2.cloned.1.call-done, f32[384,4096]{1,0:T(8,128)} %fusion.13), kind=kOutput, calls=%fused_computation.5 | convolution fusion | flops 3229089792 | bytes 16252928 | tf_op jit(solution)/shard_map/dot_general | solution.py:75
  120.7 1.2 copy-done.3
  121.8 2.1 %multiply_convert_fusion.3 = bf16[384,1024]{1,0:T(8,128)(2,1)} fusion(f32[384,1024]{1,0:T(8,128)S(1)} %fusion, bf16[1024,1024]{1,0:T(8,128)(2,1)S(1)} %copy-done, bf16[384,1024]{1,0:T(8,128)(2,1)S(1)} %copy-done.2, bf16[384]{0:T(512)(128)(2,1)S(1)} %convert_element_type.100), kind=kOutput, calls=%fused_computation.12 | convolution fusion | flops 809238528 | bytes 5243648 | tf_op jit(solution)/shard_map/dot_general | solution.py:15
  124.0 10.5 %fusion.5 = bf16[384,256]{1,0:T(8,128)(2,1)S(1)} fusion(bf16[512,4096]{1,0:T(8,128)(2,1)} %param.21, f32[384,4096]{1,0:T(8,128)} %fusion.13, bf16[384,1024]{1,0:T(8,128)(2,1)} %multiply_convert_fusion.3, bf16[4096,1024]{1,0:T(8,128)(2,1)} %all-gather.2.cloned.1.call-done), kind=kOutput, calls=%fused_computation.16 | convolution fusion | flops 4040785920 | bytes 17760256 | tf_op jit(solution)/shard_map/dot_general | solution.py:15
  134.5 10.9 %all_to_all.40 = bf16[8,48,256]{2,1,0:T(8,128)(2,1)S(1)} all-to-all(bf16[8,48,256]{2,1,0:T(8,128)(2,1)S(1)} %bitcast.162), channel_id=1, replica_groups=mesh['tower'=8,'peer'=32] {'tower'}, dimensions={0} | all-to-all | bytes 393216 | tf_op jit(solution)/shard_map/all_to_all | solution.py:89
  145.4 0.1 reshape.105
  145.5 0.3 reduce
  145.9 2.6 %fusion.2 = f32[64,2048]{1,0:T(8,128)} fusion(bf16[2048,256]{1,0:T(8,128)(2,1)} %param.20, bf16[128,256]{1,0:T(8,128)(2,1)S(1)} %reduce, s32[64]{0:T(128)S(1)} %fusion.29), kind=kOutput, calls=%fused_computation.9 | convolution fusion | flops 71606272 | bytes 1638656 | tf_op jit(solution)/shard_map/dot_general | solution.py:15
  148.4 3.1 %fusion.1 = bf16[64,2048]{1,0:T(8,128)(2,1)S(1)} fusion(bf16[2048,256]{1,0:T(8,128)(2,1)} %param.18, bf16[256,2048]{1,0:T(8,128)(2,1)} %param.19, f32[64,2048]{1,0:T(8,128)} %fusion.2, f32[64,2048]{1,0:T(8,128)S(1)} %fusion.8, bf16[64,2048]{1,0:T(8,128)(2,1)S(1)} %all_to_all.29), kind=kOutput, calls=%fused_computation.7 | convolution fusion | flops 135151616 | bytes 3670016 | tf_op jit(solution)/shard_map/dot_general | solution.py:15
  151.6 0.1 constant_dynamic-update-slice_fusion.30
  151.7 0.1 constant_dynamic-update-slice_fusion.28
  151.8 0.1 constant_dynamic-update-slice_fusion.26
  151.9 0.1 constant_dynamic-update-slice_fusion.24
  152.0 0.1 constant_dynamic-update-slice_fusion.22
  152.1 0.1 constant_dynamic-update-slice_fusion.20
  152.2 0.1 constant_dynamic-update-slice_fusion.18
  152.3 0.1 constant_dynamic-update-slice_fusion.16
  152.4 0.1 constant_dynamic-update-slice_fusion.14
  152.5 0.1 constant_dynamic-update-slice_fusion.12
  152.6 0.1 constant_dynamic-update-slice_fusion.10
  152.7 0.1 constant_dynamic-update-slice_fusion.8
  152.8 0.1 constant_dynamic-update-slice_fusion.6
  152.9 0.1 constant_dynamic-update-slice_fusion.4
  153.0 0.1 constant_dynamic-update-slice_fusion.2
  153.1 0.1 constant_dynamic-update-slice_fusion
  153.2 1.1 reshape.145
  154.3 7.6 %all-to-all-start.4 = ((bf16[32,2,2048]{2,1,0:T(2,128)(2,1)}), bf16[32,2,2048]{2,1,0:T(2,128)(2,1)S(1)}, u32[]{:S(2)}, u32[]{:S(2)}) async-start(bf16[32,2,2048]{2,1,0:T(2,128)(2,1)} %reshape.145), calls=%async_computation.4 | async-start | bytes 524288 | tf_op jit(solution)/shard_map/all_to_all | solution.py:110
  162.0 3.3 %multiply_convert_fusion.4 = bf16[384,1024]{1,0:T(8,128)(2,1)} fusion(bf16[1024,1024]{1,0:T(8,128)(2,1)S(1)} %copy-done, f32[384,1024]{1,0:T(8,128)} %copy-done.3, f32[384]{0:T(512)S(1)} %reshape.108), kind=kOutput, calls=%fused_computation.13 | convolution fusion | flops 808058880 | bytes 4457984 | tf_op jit(solution)/shard_map/dot_general | solution.py:82
  165.3 8.5 %all-to-all-done.4 = bf16[32,2,2048]{2,1,0:T(2,128)(2,1)S(1)} async-done(((bf16[32,2,2048]{2,1,0:T(2,128)(2,1)}), bf16[32,2,2048]{2,1,0:T(2,128)(2,1)S(1)}, u32[]{:S(2)}, u32[]{:S(2)}) %all-to-all-start.4) | async-done | bytes 262176 | tf_op jit(solution)/shard_map/all_to_all | solution.py:110
  173.8 0.4 reshape.146
  174.2 5.9 %scatter_custom_fusion = bf16[2048,64]{1,0:T(8,128)(2,1)S(1)} fusion(s32[2048]{0:T(1024)S(1)} %bitcast.164, bf16[2048,64]{1,0:T(8,128)(2,1)S(1)} %bitcast.161, bf16[]{:T(256)} %constant.36.clone.1), kind=kCustom, calls=%fused_computation.35 | custom fusion | bytes 262146 | tf_op jit(solution)/shard_map/scatter | solution.py:112
  180.0 0.9 copy.29
  (29 shorter events, 0.4 us)
Async XLA Ops:
  7.2 114.7 %copy-start = (bf16[1024,1024]{1,0:T(8,128)(2,1)S(1)}, bf16[1024,1024]{1,0:T(8,128)(2,1)}, u32[]{:S(2)}) copy-start(bf16[1024,1024]{1,0:T(8,128)(2,1)} %param.23) | copy-start | bytes 6291460
  7.2 105.4 %all-gather.2.cloned.1.call-start = ((), (), s32[]{:S(2)}) async-start(), calls=%async_computation.5 | async-start | bytes 8650752 | tf_op jit(solution)/shard_map/all_gather | solution.py:77
  11.7 15.8 %all-to-all-start.2 = ((s32[8,1,16]{2,1,0:T(1,128)}), s32[8,1,16]{2,1,0:T(1,128)S(1)}, u32[]{:S(2)}, u32[]{:S(2)}) async-start(s32[8,1,16]{2,1,0:T(1,128)} %bitcast.8), calls=%async_computation.2 | async-start | bytes 8192 | tf_op jit(solution)/shard_map/all_to_all | solution.py:63
  27.4 26.5 %all-to-all-start = ((bf16[32,2,2048]{2,1,0:T(2,128)(2,1)}), bf16[32,2,2048]{2,1,0:T(2,128)(2,1)S(1)}, u32[]{:S(2)}, u32[]{:S(2)}) async-start(bf16[32,2,2048]{2,1,0:T(2,128)(2,1)} %reshape.143), calls=%async_computation | async-start | bytes 524288 | tf_op jit(solution)/shard_map/all_to_all | solution.py:40
  55.1 16.3 %copy-start.1 = (bf16[384,256]{1,0:T(8,128)(2,1)S(1)}, bf16[384,256]{1,0:T(8,128)(2,1)}, u32[]{:S(2)}) copy-start(bf16[384,256]{1,0:T(8,128)(2,1)} %param.16) | copy-start | bytes 589828
  60.1 11.3 %all-to-all-start.1 = ((bf16[8,48,256]{2,1,0:T(8,128)(2,1)}), bf16[8,48,256]{2,1,0:T(8,128)(2,1)S(1)}, u32[]{:S(2)}, u32[]{:S(2)}) async-start(bf16[8,48,256]{2,1,0:T(8,128)(2,1)} %reshape.102), calls=%async_computation.1 | async-start | bytes 393216 | tf_op jit(solution)/shard_map/all_to_all | solution.py:62
  112.5 9.3 %copy-start.2 = (bf16[384,1024]{1,0:T(8,128)(2,1)S(1)}, bf16[384,1024]{1,0:T(8,128)(2,1)}, u32[]{:S(2)}) copy-start(bf16[384,1024]{1,0:T(8,128)(2,1)} %param.17) | copy-start | bytes 2359300
  120.7 1.2 copy-start.3
  154.3 19.5 %all-to-all-start.4 = ((bf16[32,2,2048]{2,1,0:T(2,128)(2,1)}), bf16[32,2,2048]{2,1,0:T(2,128)(2,1)S(1)}, u32[]{:S(2)}, u32[]{:S(2)}) async-start(bf16[32,2,2048]{2,1,0:T(2,128)(2,1)} %reshape.145), calls=%async_computation.4 | async-start | bytes 524288 | tf_op jit(solution)/shard_map/all_to_all | solution.py:110
Sparse Core Ops, SparseCore 0:
  10.6 101.8 all-gather.1
